TPU v7x, 256 devices: a whole 4x4x8 slice. The times are simulated.
256 devices in a mesh: inst: 16 (over z, x_hi), tp: 16 (over x_lo, y, core).
Axes of the slice: x: 4 (x_hi: 2, x_lo: 2; x = x_hi * 2 + x_lo), y: 4, z: 8, core: 2. Of those that a mesh axis runs over, the one named last changes fastest.
Arguments:
- tokens: bfloat16 [16384, 4608], P(('inst', 'tp')), may hold values from -6 to 6
- w_query: bfloat16 [4608, 4096], P(None, 'tp'), may hold values from -0.09375 to 0.09375
- w_keyval: bfloat16 [4608, 4096], P(None, 'tp'), may hold values from -0.09375 to 0.09375
- w_out: bfloat16 [4096, 4608], P('tp'), may hold values from -0.09375 to 0.09375
- kv_pool: bfloat16 [512, 256, 4096], P('inst', None, 'tp'), may hold values from -6 to 6
- req_target: int32 [16, 16], P('inst'), may hold values from 0 to 15, each once within a row
- page_counts: int32 [16, 16], P('inst'), may hold values from 1 to 4, 32 in all within a row
- tail_tokens: int32 [16, 16], P('inst'), may hold values from 1 to 256
- migrate: int32 [16, 16], P('inst'), may hold values 0 or 1
- pool_order: int32 [16, 32], P('inst'), may hold values from 0 to 31, each once within a row
Outputs:
- attn_out: bfloat16 [16384, 4608], P(('inst', 'tp'))
Inputs may be any that keep to these rules, and one draw needn't show every extreme that they name: `req_target`: each row is a permutation: every source sends exactly one request to every target instance. `page_counts`: each source's requests hold all of its 32 pages together, and some request of every source holds 4 pages. `pool_order`: each row is a permutation of the source's pages.
All inputs are finite; a program needn't handle non-finite values. No bound on the sum of `migrate` on one device may be relied on, other than what follows from the above.
Results may differ from a plain program's by a relative error of at most 0.023.
Values may be sent and summed in bfloat16 or wider, within the bound.
A program may use at most 128 MiB of HBM per device.

v0:
```python
import jax
import jax.numpy as jnp
from jax import lax
from jax.sharding import PartitionSpec as P

D = 4608
HEADS = 32
HD = 128
PAGE = 256
PPR = 4


SOFTCAP = 50.0
ROPE_BASE = 10000.0


def rotate(vectors, positions):
    head_dim = vectors.shape[-1]
    half_dim = head_dim // 2
    frequency = ROPE_BASE ** (-2.0 * jnp.arange(half_dim, dtype=jnp.float32) / head_dim)
    angles = positions.astype(jnp.float32)[:, None] * frequency[None, :]
    cosine = jnp.cos(angles)[:, None, :]
    sines = jnp.sin(angles)[:, None, :]
    leading = vectors[..., :half_dim]
    trailing = vectors[..., half_dim:]
    return jnp.concatenate(
        [leading * cosine - trailing * sines, trailing * cosine + leading * sines], axis=-1
    )


def capped_weights(scores):
    return jnp.exp(SOFTCAP * jnp.tanh(scores / SOFTCAP) - SOFTCAP)


def source_tables(targets, counts, tail_len, flag_set, pool_order):
    number = targets.shape[0]
    matches = (targets[:, None] == jnp.arange(number, dtype=jnp.int32)[None, :]).astype(jnp.int32)
    starts = jnp.cumsum(counts) - counts

    def pick(column):
        return jnp.sum(column[:, None] * matches, axis=0)

    count_to = pick(counts)
    cached = pick(flag_set) * ((count_to - 1) * PAGE + pick(tail_len))
    slots = pick(starts)[:, None] + jnp.arange(PPR, dtype=jnp.int32)[None, :]
    slots = jnp.minimum(slots, pool_order.shape[0] - 1)
    return (cached, pool_order[slots])


def block_part(queries, keys, values, score_scale):
    scores = (
        jnp.einsum("nihgd,njhd->nhgij", queries, keys, preferred_element_type=jnp.float32)
        * score_scale
    )
    length = queries.shape[1]
    causal = jnp.arange(length)[:, None] >= jnp.arange(length)[None, :]
    softmax_w = jnp.where(causal, capped_weights(scores), 0.0)
    totals = jnp.transpose(jnp.sum(softmax_w, axis=-1), (0, 3, 1, 2))
    weighted = jnp.einsum(
        "nhgij,njhd->nihgd",
        softmax_w.astype(jnp.bfloat16),
        values,
        preferred_element_type=jnp.float32,
    )
    return (totals, weighted)


def cache_part(queries, cache_pages, cached, score_scale):
    shape_in = cache_pages.shape
    heads = queries.shape[2]
    head_dim = queries.shape[4]
    stacked = cache_pages.reshape(shape_in[0], shape_in[1] * shape_in[2], heads, 2, head_dim)
    keys = stacked[:, :, :, 0]
    values = stacked[:, :, :, 1]
    scores = (
        jnp.einsum("nihgd,nchd->nhgic", queries, keys, preferred_element_type=jnp.float32)
        * score_scale
    )
    live_mask = jnp.arange(keys.shape[1])[None, :] < cached[:, None]
    softmax_w = jnp.where(live_mask[:, None, None, None, :], capped_weights(scores), 0.0)
    totals = jnp.transpose(jnp.sum(softmax_w, axis=-1), (0, 3, 1, 2))
    weighted = jnp.einsum(
        "nhgic,nchd->nihgd",
        softmax_w.astype(jnp.bfloat16),
        values,
        preferred_element_type=jnp.float32,
    )
    return (totals, weighted)


def shards(
    tokens,
    w_query,
    w_keyval,
    w_out,
    kv_pool,
    req_target,
    page_counts,
    tail_tokens,
    migrate,
    pool_order,
):
    instances = lax.axis_size("inst")
    query_width = w_query.shape[1]
    local_heads = w_keyval.shape[1] // (2 * HD)
    groups = query_width // (local_heads * HD)
    row_count = tokens.shape[0] * lax.axis_size("tp")
    per_request = row_count // instances
    score_scale = (D // HEADS) ** (-0.5)
    cached_out, page_ids = source_tables(
        req_target[0], page_counts[0], tail_tokens[0], migrate[0], pool_order[0]
    )
    arrived, cached = (
        lax.all_to_all(kv_pool[page_ids], "inst", split_axis=0, concat_axis=0, tiled=True),
        lax.all_to_all(cached_out, "inst", split_axis=0, concat_axis=0, tiled=True),
    )
    piece = lax.all_gather(tokens, "tp", axis=0, tiled=True)
    projected = jnp.concatenate(
        [
            jnp.dot(piece, w_query, preferred_element_type=jnp.float32),
            jnp.dot(piece, w_keyval, preferred_element_type=jnp.float32),
        ],
        axis=1,
    )
    positions = (cached[:, None] + jnp.arange(per_request, dtype=jnp.int32)[None, :]).reshape(
        row_count
    )
    queries = rotate(
        projected[:, :query_width].reshape(row_count, local_heads * groups, HD), positions
    ).astype(jnp.bfloat16)
    keyval = projected[:, query_width:].reshape(row_count, local_heads, 2, HD)
    keys = rotate(keyval[:, :, 0], positions).astype(jnp.bfloat16)
    values = keyval[:, :, 1].astype(jnp.bfloat16)
    queries = queries.reshape(instances, per_request, local_heads, groups, HD)
    keys = keys.reshape(instances, per_request, local_heads, HD)
    values = values.reshape(instances, per_request, local_heads, HD)
    totals, weighted = block_part(queries, keys, values, score_scale)
    far_totals, far_weighted = cache_part(queries, arrived, cached, score_scale)
    attended = ((weighted + far_weighted) / (totals + far_totals)[..., None]).astype(jnp.bfloat16)
    attended = attended.reshape(row_count, query_width)
    return lax.psum_scatter(
        jnp.dot(attended, w_out, preferred_element_type=jnp.float32).astype(jnp.bfloat16),
        "tp",
        scatter_dimension=0,
        tiled=True,
    )


def solution(mesh):
    return jax.shard_map(
        shards,
        mesh=mesh,
        in_specs=(
            P(("inst", "tp"), None),
            P(None, "tp"),
            P(None, "tp"),
            P("tp", None),
            P("inst", None, "tp"),
            P("inst", None),
            P("inst", None),
            P("inst", None),
            P("inst", None),
            P("inst", None),
        ),
        out_specs=P(("inst", "tp"), None),
        check_vma=False,
    )
```

profile of v0, /device:TPU:32, one launch (start us, length us, event | category | flops | bytes accessed | tf_op | source)
XLA Modules:
  0.0 394.9 jit_solution(8622050592761278015)
XLA Ops:
  6.5 0.0 copy-start
  6.5 0.9 copy.55
  7.5 0.1 reduce.3
  7.6 0.7 bitcast_subtract_fusion
  8.2 0.8 select_reduce_fusion.2
  9.0 0.7 copy.49
  9.7 11.0 %all-to-all-start = ((s32[16,1,1]{2,1,0:T(1,128)}), s32[16,1,1]{2,1,0:T(1,128)S(1)}, u32[]{:S(2)}, u32[]{:S(2)}) async-start(s32[16,1,1]{2,1,0:T(1,128)} %copy.49), calls=%async_computation | async-start | bytes 16384 | tf_op jit(solution)/shard_map/all_to_all | solution.py:115
  20.8 0.1 compare_select_fusion.1
  20.8 0.1 reshape.363
  20.9 1.4 gather_fusion
  22.4 0.1 gather.9
  22.5 0.1 reshape.371
  22.6 7.8 %gather_fusion.1 = bf16[64,256,256]{2,1,0:T(8,128)(2,1)} fusion(bf16[32,256,256]{2,1,0:T(8,128)(2,1)} %param.14, s32[1024]{0:T(1024)S(1)} %pad_clamp_fusion), kind=kCustom, calls=%fused_computation.1 | custom fusion | bytes 16777472 | tf_op jit(solution)/shard_map/gather | solution.py:114
  30.4 0.0 all-to-all-done
  30.4 9.6 %all-to-all-start.1 = ((bf16[16,4,256,256]{3,2,1,0:T(8,128)(2,1)}), bf16[16,4,256,256]{3,2,1,0:T(8,128)(2,1)}, u32[]{:S(2)}, u32[]{:S(2)}) async-start(bf16[16,4,256,256]{3,2,1,0:T(8,128)(2,1)} %bitcast.106), calls=%async_computation.1 | async-start | bytes 16777216 | tf_op jit(solution)/shard_map/all_to_all | solution.py:114
  40.0 0.0 all-gather.2.cloned.1.call-start
  40.1 0.7 all-gather.2.cloned.1.call-update
  40.8 0.0 reduce-scatter.2.cloned.1.call-start
  40.9 0.4 reduce.2
  41.2 0.1 add_convert_fusion.1
  41.3 0.1 convert_element_type.43
  41.4 0.1 iota_compare_fusion
  41.5 1.0 multiply_cosine_fusion
  42.5 189.0 %all-to-all-done.1 = bf16[16,4,256,256]{3,2,1,0:T(8,128)(2,1)} async-done(((bf16[16,4,256,256]{3,2,1,0:T(8,128)(2,1)}), bf16[16,4,256,256]{3,2,1,0:T(8,128)(2,1)}, u32[]{:S(2)}, u32[]{:S(2)}) %all-to-all-start.1) | async-done | bytes 8388640 | tf_op jit(solution)/shard_map/all_to_all | solution.py:114
  231.5 12.5 %reshape.350 = bf16[16,1024,1,2,128]{4,3,1,0,2:T(2,128)(2,1)} reshape(bf16[16,4,256,256]{3,2,1,0:T(8,128)(2,1)} %all-to-all-done.1) | data formatting | bytes 16777216 | tf_op jit(solution)/shard_map/reshape | solution.py:72
  244.0 17.7 %fusion.35 = (bf16[16,1024,1,1,128]{4,3,1,0,2:T(2,128)(2,1)}, bf16[16,1024,1,1,128]{4,3,1,0,2:T(2,128)(2,1)}) fusion(bf16[16,1024,1,2,128]{4,3,1,0,2:T(2,128)(2,1)} %reshape.350), kind=kLoop, calls=%fused_computation.71 | loop fusion | bytes 16777216 | tf_op jit(solution)/shard_map/slice | solution.py:73
  261.7 0.0 all-gather.2.cloned.1.call-done
  261.7 0.0 copy-start.5
  261.7 0.0 copy-start.6
  261.7 6.2 %fusion.37 = f32[1024,256]{0,1:T(8,128)S(1)} fusion(bf16[1024,4608]{1,0:T(8,128)(2,1)} %all-gather.2.cloned.1.call-done, bf16[4608,256]{1,0:T(8,128)(2,1)} %param.12), kind=kOutput, calls=%fused_computation.73 | convolution fusion | flops 2415919104 | bytes 12845056 | tf_op jit(solution)/shard_map/dot_general | solution.py:121
  267.9 0.7 slice.55
  268.7 0.1 copy-done.5
  268.8 0.8 copy-done.6
  269.6 2.6 fusion.38
  272.2 1.0 subtract_convert_fusion
  273.2 1.3 concatenate.26
  274.5 1.3 copy.52
  275.8 1.1 fusion.24
  277.0 1.8 copy.48
  278.8 0.9 copy.50
  279.6 0.8 copy.51
  280.5 1.3 concatenate.27
  281.8 0.5 copy.53
  282.3 10.1 %bitcast_reduce_fusion = (f32[16,2,64]{2,1,0:T(2,128)S(1)}, f32[16,1024,64,2]{1,2,3,0:T(8,128)}) fusion(pred[16,1024]{1,0:T(8,128)(4,1)S(1)} %iota_compare_fusion, bf16[16,64,2,64]{3,1,2,0:T(8,128)(2,1)S(1)} %copy.53, bf16[16,64,2,64]{3,1,2,0:T(8,128)(2,1)} %copy.52, bf16[16,1024,1,1,128]{4,3,1,0,2:T(2,128)(2,1)} %get-tuple-element.9), kind=kOutput, calls=%fused_computation.3 | convolution fusion | flops 548403200 | bytes 13131776 | tf_op jit(solution)/shard_map/nihgd,nchd->nhgic/dot_general | solution.py:76
  292.4 0.0 copy-start.1
  292.4 0.0 copy-start.2
  292.4 0.0 copy-start.3
  292.4 0.0 copy-start.4
  292.4 9.8 %fusion.2 = f32[16,128,2,64]{1,3,2,0:T(8,128)S(1)} fusion(bf16[16,1024,1,1,128]{4,3,1,0,2:T(2,128)(2,1)} %get-tuple-element.10, f32[16,1024,64,2]{1,2,3,0:T(8,128)} %get-tuple-element.20, pred[16,1024]{1,0:T(8,128)(4,1)S(1)} %iota_compare_fusion), kind=kOutput, calls=%fused_computation.10 | convolution fusion | flops 547356672 | bytes 13647872 | tf_op jit(solution)/shard_map/nhgic,nchd->nihgd/dot_general | solution.py:82
  302.2 0.0 copy-done.1
  302.2 0.0 copy-done.2
  302.2 0.0 copy-done.3
  302.2 0.9 fusion.36
  303.2 0.0 copy-done.4
  303.2 0.5 divide_convert_fusion
  303.7 0.5 copy.58
  304.3 0.0 copy-done
  304.3 5.0 %convolution_convert_fusion = bf16[1024,4608]{1,0:T(8,128)(2,1)} fusion(bf16[256,4608]{1,0:T(8,128)(2,1)S(1)} %copy-done, bf16[128,8,2,128]{3,2,1,0:T(2,128)(2,1)S(1)} %bitcast.107), kind=kOutput, calls=%fused_computation.2 | convolution fusion | flops 2420637696 | bytes 12320768 | tf_op jit(solution)/shard_map/dot_general | solution.py:142
  309.3 0.0 reduce-scatter.2.cloned.1.call-update
  309.3 78.8 %reduce-scatter.2.cloned.1.call-done = bf16[64,4608]{1,0:T(8,128)(2,1)} async-done(((bf16[1024,4608]{1,0:T(8,128)(2,1)}), bf16[64,4608]{1,0:T(8,128)(2,1)}) %reduce-scatter.2.cloned.1.call-update) | async-done | bytes 589840 | tf_op jit(solution)/shard_map/reduce_scatter | solution.py:141
  (9 shorter events, 0.1 us)
Async XLA Ops:
  6.5 297.7 %copy-start = (bf16[256,4608]{1,0:T(8,128)(2,1)S(1)}, bf16[256,4608]{1,0:T(8,128)(2,1)}, u32[]{:S(2)}) copy-start(bf16[256,4608]{1,0:T(8,128)(2,1)} %param.13) | copy-start | bytes 7077892
  9.7 20.7 %all-to-all-start = ((s32[16,1,1]{2,1,0:T(1,128)}), s32[16,1,1]{2,1,0:T(1,128)S(1)}, u32[]{:S(2)}, u32[]{:S(2)}) async-start(s32[16,1,1]{2,1,0:T(1,128)} %copy.49), calls=%async_computation | async-start | bytes 16384 | tf_op jit(solution)/shard_map/all_to_all | solution.py:115
  30.4 201.1 %all-to-all-start.1 = ((bf16[16,4,256,256]{3,2,1,0:T(8,128)(2,1)}), bf16[16,4,256,256]{3,2,1,0:T(8,128)(2,1)}, u32[]{:S(2)}, u32[]{:S(2)}) async-start(bf16[16,4,256,256]{3,2,1,0:T(8,128)(2,1)} %bitcast.106), calls=%async_computation.1 | async-start | bytes 16777216 | tf_op jit(solution)/shard_map/all_to_all | solution.py:114
  40.0 221.7 %all-gather.2.cloned.1.call-start = ((), (), s32[]{:S(2)}) async-start(), calls=%async_computation.3 | async-start | bytes 10027008 | tf_op jit(solution)/shard_map/all_gather | solution.py:117
  40.8 347.3 %reduce-scatter.2.cloned.1.call-start = ((), (), s32[]{:S(2)}) async-start(), calls=%async_computation.4 | async-start | bytes 10027008 | tf_op jit(solution)/shard_map/reduce_scatter | solution.py:141
  261.7 7.1 %copy-start.5 = (bf16[1024,4608]{1,0:T(8,128)(2,1)S(1)}, bf16[1024,4608]{1,0:T(8,128)(2,1)}, u32[]{:S(2)}) copy-start(bf16[1024,4608]{1,0:T(8,128)(2,1)} %all-gather.2.cloned.1.call-done) | copy-start | bytes 28311556
  261.7 7.9 %copy-start.6 = (bf16[4608,256]{1,0:T(8,128)(2,1)S(1)}, bf16[4608,256]{1,0:T(8,128)(2,1)}, u32[]{:S(2)}) copy-start(bf16[4608,256]{1,0:T(8,128)(2,1)} %param.11) | copy-start | bytes 7077892
  292.4 9.8 %copy-start.1 = (bf16[16,64,2,64]{3,1,2,0:T(8,128)(2,1)S(1)}, bf16[16,64,2,64]{3,1,2,0:T(8,128)(2,1)}, u32[]{:S(2)}) copy-start(bf16[16,64,2,64]{3,1,2,0:T(8,128)(2,1)} %copy.52) | copy-start | bytes 786436
  292.4 9.8 %copy-start.2 = (bf16[1024,1,64]{2,0,1:T(8,128)(2,1)S(1)}, bf16[1024,1,64]{2,0,1:T(8,128)(2,1)}, u32[]{:S(2)}) copy-start(bf16[1024,1,64]{2,0,1:T(8,128)(2,1)} %copy.50) | copy-start | bytes 393220
  292.4 9.8 %copy-start.3 = (bf16[1024,1,64]{2,0,1:T(8,128)(2,1)S(1)}, bf16[1024,1,64]{2,0,1:T(8,128)(2,1)}, u32[]{:S(2)}) copy-start(bf16[1024,1,64]{2,0,1:T(8,128)(2,1)} %copy.51) | copy-start | bytes 393220
  292.4 10.7 %copy-start.4 = (bf16[1024,1,1,128]{3,0,2,1:T(8,128)(2,1)S(1)}, bf16[1024,1,1,128]{3,0,2,1:T(8,128)(2,1)}, u32[]{:S(2)}) copy-start(bf16[1024,1,1,128]{3,0,2,1:T(8,128)(2,1)} %copy.48) | copy-start | bytes 786436
Sparse Core Ops, SparseCore 0:
  42.7 60.7 all-gather.1
  309.4 78.6 reduce-scatter.1
where the time goes:
time: 396 us; the launch traced here: 395 us
  waiting for transfers between devices  269 us (68%)
  local copies, waits for them, and re-layouts  51.5 us (13%)
  matrix products  35.1 us (9%)
  starting transfers between devices  20.8 us (5%)
  between operations  13.7 us (3%)
  other arithmetic  5.38 us (1%)
    all_to_all x1, waiting for transfers between devices, shards(): lax.all_to_all(kv_pool[page_ids], 'inst', split_axis=0, concat_axis=0, ti...  189 us
    reduce_scatter x1, waiting for transfers between devices, shards(): lax.psum_scatter(jnp.dot(attended, w_out, preferred_element_type=jnp.floa...  78.8 us
    slice x1, local copies, waits for them, and re-layouts, cache_part(): keys = stacked[:, :, :, 0]  17.7 us
    reshape x1, local copies, waits for them, and re-layouts, cache_part(): cache_pages.reshape(shape_in[0], shape_in[1] * shape_in[2], heads, 2, hea...  12.5 us
    all_to_all x1, starting transfers between devices, shards(): lax.all_to_all(cached_out, 'inst', split_axis=0, concat_axis=0, tiled=True)  11 us
    dot_general x1, matrix products, cache_part(): jnp.einsum('nihgd,nchd->nhgic', queries, keys, preferred_element_type=jnp...  10.1 us
    dot_general x1, matrix products, cache_part(): jnp.einsum('nhgic,nchd->nihgd', softmax_w.astype(jnp.bfloat16), values, p...  9.76 us
    all_to_all x1, starting transfers between devices, shards(): lax.all_to_all(kv_pool[page_ids], 'inst', split_axis=0, concat_axis=0, ti...  9.63 us
  transfers between devices with their start and end apart: 4, of which 2 were waited for; matrix products, arithmetic and copies ran while one was open for 10% of the time, Pallas kernels for 0%

commit v1 on v0

--- a/solution.py
+++ b/solution.py
@@ -110,10 +110,7 @@
     cached_out, page_ids = source_tables(
         req_target[0], page_counts[0], tail_tokens[0], migrate[0], pool_order[0]
     )
-    arrived, cached = (
-        lax.all_to_all(kv_pool[page_ids], "inst", split_axis=0, concat_axis=0, tiled=True),
-        lax.all_to_all(cached_out, "inst", split_axis=0, concat_axis=0, tiled=True),
-    )
+    near = jnp.tile(jnp.arange(per_request, dtype=jnp.int32), instances)
     piece = lax.all_gather(tokens, "tp", axis=0, tiled=True)
     projected = jnp.concatenate(
         [
@@ -122,20 +119,34 @@
         ],
         axis=1,
     )
-    positions = (cached[:, None] + jnp.arange(per_request, dtype=jnp.int32)[None, :]).reshape(
-        row_count
-    )
     queries = rotate(
-        projected[:, :query_width].reshape(row_count, local_heads * groups, HD), positions
+        projected[:, :query_width].reshape(row_count, local_heads * groups, HD), near
     ).astype(jnp.bfloat16)
     keyval = projected[:, query_width:].reshape(row_count, local_heads, 2, HD)
-    keys = rotate(keyval[:, :, 0], positions).astype(jnp.bfloat16)
+    keys = rotate(keyval[:, :, 0], near).astype(jnp.bfloat16)
     values = keyval[:, :, 1].astype(jnp.bfloat16)
+    there = lax.all_to_all(
+        queries.reshape(instances, per_request, query_width),
+        "inst", split_axis=0, concat_axis=0, tiled=True,
+    )
+    offsets = jnp.repeat(cached_out, per_request)
+    there = rotate(
+        there.reshape(row_count, local_heads * groups, HD).astype(jnp.float32), offsets
+    ).astype(jnp.bfloat16)
+    there = there.reshape(instances, per_request, local_heads, groups, HD)
+    far_totals, far_weighted = cache_part(there, kv_pool[page_ids], cached_out, score_scale)
+    far_weighted = lax.all_to_all(
+        far_weighted.astype(jnp.bfloat16).reshape(instances, per_request, query_width),
+        "inst", split_axis=0, concat_axis=0, tiled=True,
+    ).reshape(instances, per_request, local_heads, groups, HD).astype(jnp.float32)
+    far_totals = lax.all_to_all(
+        far_totals.reshape(instances, per_request * local_heads * groups),
+        "inst", split_axis=0, concat_axis=0, tiled=True,
+    ).reshape(instances, per_request, local_heads, groups)
     queries = queries.reshape(instances, per_request, local_heads, groups, HD)
     keys = keys.reshape(instances, per_request, local_heads, HD)
     values = values.reshape(instances, per_request, local_heads, HD)
     totals, weighted = block_part(queries, keys, values, score_scale)
-    far_totals, far_weighted = cache_part(queries, arrived, cached, score_scale)
     attended = ((weighted + far_weighted) / (totals + far_totals)[..., None]).astype(jnp.bfloat16)
     attended = attended.reshape(row_count, query_width)
     return lax.psum_scatter(

time: 396 us -> 285 us (0.72)
  waiting for transfers between devices: 269 us -> 115 us
  local copies, waits for them, and re-layouts: 51.5 us -> 72.4 us
  starting transfers between devices: 20.8 us -> 29.2 us
  other arithmetic: 5.38 us -> 12.6 us
  matrix products: 35.1 us -> 40 us
    all_to_all x2 -> x3, waiting for transfers between devices: 189 us -> 0.01 us  [the longest x1 0.01 us: shards(): lax.all_to_all(queries.reshape(instances, per_request, query_width), 'ins...]
    all_gather x1, waiting for transfers between devices: 0.02 us -> 34.6 us  [shards(): piece = lax.all_gather(tokens, 'tp', axis=0, tiled=True)]
    all_to_all x2 -> x3, starting transfers between devices: 20.7 us -> 29.2 us  [the longest x1 9.92 us: shards(): lax.all_to_all(queries.reshape(instances, per_request, query_width), 'ins...]
    unnamed x14 -> x16, local copies, waits for them, and re-layouts: 0.92 us -> 8.42 us
    convert_element_type x0 -> x4, local copies, waits for them, and re-layouts: none -> 4.77 us  [the longest x1 1.55 us: shards(): there.reshape(row_count, local_heads * groups, HD).astype(jnp.float32)]
    another operation x4 -> x5, other arithmetic: 2.28 us -> 6.25 us
    slice x1 -> x3, local copies, waits for them, and re-layouts: 17.7 us -> 20.7 us  [the longest x1 17.2 us: cache_part(): values = stacked[:, :, :, 1]]
  transfers between devices with their start and end apart: 4 -> 5, of which waited for: 2 -> 2; matrix products, arithmetic and copies ran while one was open for 10% -> 26% of each run, Pallas kernels for 0% -> 0%
where the time goes in v1:
time: 285 us; the launch traced here: 283 us
  waiting for transfers between devices  115 us (40%)
  local copies, waits for them, and re-layouts  72.4 us (25%)
  matrix products  40 us (14%)
  starting transfers between devices  29.2 us (10%)
  between operations  13.7 us (5%)
  other arithmetic  12.6 us (4%)
    reduce_scatter x1, waiting for transfers between devices, shards(): lax.psum_scatter(jnp.dot(attended, w_out, preferred_element_type=jnp.floa...  80.1 us
    all_gather x1, waiting for transfers between devices, shards(): piece = lax.all_gather(tokens, 'tp', axis=0, tiled=True)  34.6 us
    slice x1, local copies, waits for them, and re-layouts, cache_part(): values = stacked[:, :, :, 1]  17.2 us
    reshape x1, local copies, waits for them, and re-layouts, cache_part(): cache_pages.reshape(shape_in[0], shape_in[1] * shape_in[2], heads, 2, hea...  12.6 us
    dot_general x1, matrix products, cache_part(): jnp.einsum('nihgd,nchd->nhgic', queries, keys, preferred_element_type=jnp...  10.2 us
    all_to_all x1, starting transfers between devices, shards(): lax.all_to_all(queries.reshape(instances, per_request, query_width), 'ins...  9.92 us
    all_to_all x1, starting transfers between devices, shards(): lax.all_to_all(far_totals.reshape(instances, per_request * local_heads *...  9.64 us
    all_to_all x1, starting transfers between devices, shards(): lax.all_to_all(far_weighted.astype(jnp.bfloat16).reshape(instances, per_r...  9.63 us
  transfers between devices with their start and end apart: 5, of which 2 were waited for; matrix products, arithmetic and copies ran while one was open for 26% of the time, Pallas kernels for 0%

profile of v1, /device:TPU:32, one launch (start us, length us, event | category | flops | bytes accessed | tf_op | source)
XLA Modules:
  0.0 283.4 jit_solution(15222423012681047064)
XLA Ops:
  6.5 0.7 all-gather.2.cloned.1.call-update
  7.3 0.7 copy.100
  8.0 0.1 reduce.2
  8.1 0.7 bitcast_subtract_fusion
  8.8 0.8 select_reduce_fusion.1
  9.8 0.1 compare_select_fusion.1
  9.8 0.1 reshape.426
  9.9 1.4 gather_fusion
  11.4 0.1 gather.9
  11.5 0.1 reshape.434
  11.7 2.7 multiply_cosine_fusion
  14.4 1.0 copy.94
  15.4 1.0 copy.92
  16.4 7.8 %gather_fusion.1 = bf16[64,256,256]{2,1,0:T(8,128)(2,1)} fusion(bf16[32,256,256]{2,1,0:T(8,128)(2,1)} %param.14, s32[1024]{0:T(1024)S(1)} %pad_clamp_fusion), kind=kCustom, calls=%fused_computation.1 | custom fusion | bytes 16777472 | tf_op jit(solution)/shard_map/gather | solution.py:137
  24.2 12.6 %reshape.448 = bf16[16,1024,1,2,128]{4,3,1,0,2:T(2,128)(2,1)} reshape(bf16[64,256,256]{2,1,0:T(8,128)(2,1)} %gather_fusion.1) | data formatting | bytes 16777216 | tf_op jit(solution)/shard_map/reshape | solution.py:72
  36.8 34.6 %all-gather.2.cloned.1.call-done = bf16[1024,4608]{1,0:T(8,128)(2,1)} async-done(((bf16[64,4608]{1,0:T(8,128)(2,1)}), bf16[1024,4608]{1,0:T(8,128)(2,1)}) %all-gather.2.cloned.1.call-update) | async-done | bytes 9437200 | tf_op jit(solution)/shard_map/all_gather | solution.py:114
  71.4 6.0 %fusion.56 = f32[1024,256]{0,1:T(8,128)S(1)} fusion(bf16[1024,4608]{1,0:T(8,128)(2,1)} %all-gather.2.cloned.1.call-done, bf16[4608,256]{1,0:T(8,128)(2,1)} %param.11), kind=kOutput, calls=%fused_computation.91 | convolution fusion | flops 2415919104 | bytes 12845056 | tf_op jit(solution)/shard_map/dot_general | solution.py:117
  77.4 1.1 fusion.53
  78.5 1.4 copy.128
  80.0 2.1 copy.127
  82.1 2.3 subtract_convert_fusion
  84.5 0.8 copy-done.1
  85.2 0.2 copy-done.3
  85.4 1.4 pad_maximum_fusion
  86.9 1.1 convert_element_type.119
  88.0 9.9 %all-to-all-start = ((bf16[16,64,256]{2,1,0:T(8,128)(2,1)}), bf16[16,64,256]{2,1,0:T(8,128)(2,1)}, u32[]{:S(2)}, u32[]{:S(2)}) async-start(bf16[16,64,256]{2,1,0:T(8,128)(2,1)} %convert_element_type.119), calls=%async_computation | async-start | bytes 1048576 | tf_op jit(solution)/shard_map/all_to_all | solution.py:128
  97.9 17.2 %fusion.51 = (bf16[16,1024,1,1,128]{4,3,1,0,2:T(2,128)(2,1)}, bf16[16,1024,1,1,128]{4,3,1,0,2:T(2,128)(2,1)}) fusion(bf16[16,1024,1,2,128]{4,3,1,0,2:T(2,128)(2,1)} %reshape.448), kind=kLoop, calls=%fused_computation.86 | loop fusion | bytes 16777216 | tf_op jit(solution)/shard_map/slice | solution.py:74
  115.1 0.6 iota_compare_fusion.1
  115.7 0.1 iota_compare_fusion
  115.8 1.5 reshape.418
  117.4 2.5 fusion.52
  119.8 1.4 copy.132
  121.2 1.4 copy.131
  122.7 2.0 subtract_convert_fusion.1
  124.7 1.3 concatenate.42
  126.0 0.5 copy.106
  126.5 1.3 concatenate.43
  127.9 1.3 copy.107
  129.1 10.2 %bitcast_reduce_fusion = (f32[16,2,64]{2,1,0:T(2,128)S(1)}, f32[16,1024,64,2]{1,2,3,0:T(8,128)}) fusion(pred[16,1024]{1,0:T(8,128)(4,1)S(1)} %iota_compare_fusion, bf16[16,64,2,64]{3,1,2,0:T(8,128)(2,1)} %copy.107, bf16[16,64,2,64]{3,1,2,0:T(8,128)(2,1)S(1)} %copy.106, bf16[16,1024,1,1,128]{4,3,1,0,2:T(2,128)(2,1)} %get-tuple-element.12), kind=kOutput, calls=%fused_computation.3 | convolution fusion | flops 548403200 | bytes 13131776 | tf_op jit(solution)/shard_map/nihgd,nchd->nhgic/dot_general | solution.py:76
  139.4 0.1 copy.110
  139.5 0.7 copy.111
  140.1 9.6 %all-to-all-start.2 = ((f32[16,1,128]{2,1,0:T(1,128)}), f32[16,1,128]{2,1,0:T(1,128)S(1)}, u32[]{:S(2)}, u32[]{:S(2)}) async-start(f32[16,1,128]{2,1,0:T(1,128)} %copy.111), calls=%async_computation.2 | async-start | bytes 16384 | tf_op jit(solution)/shard_map/all_to_all | solution.py:142
  149.8 8.3 %fusion.20 = bf16[16,64,1,2,128]{4,1,3,0,2:T(8,128)(2,1)S(1)} fusion(f32[16,1024,64,2]{1,2,3,0:T(8,128)} %get-tuple-element.30, pred[16,1024]{1,0:T(8,128)(4,1)S(1)} %iota_compare_fusion, bf16[16,1024,1,1,128]{4,3,1,0,2:T(2,128)(2,1)} %get-tuple-element.11), kind=kOutput, calls=%fused_computation.27 | convolution fusion | flops 547618816 | bytes 13123584 | tf_op jit(solution)/shard_map/nhgic,nchd->nihgd/dot_general | solution.py:82
  158.1 0.5 copy.108
  158.7 1.1 reshape.413
  159.8 9.6 %all-to-all-start.1 = ((bf16[16,64,256]{2,1,0:T(8,128)(2,1)}), bf16[16,64,256]{2,1,0:T(8,128)(2,1)}, u32[]{:S(2)}, u32[]{:S(2)}) async-start(bf16[16,64,256]{2,1,0:T(8,128)(2,1)} %reshape.413), calls=%async_computation.1 | async-start | bytes 1048576 | tf_op jit(solution)/shard_map/all_to_all | solution.py:138
  169.5 6.1 %fusion.55 = f32[1024,256]{0,1:T(8,128)S(1)} fusion(bf16[1024,4608]{1,0:T(8,128)(2,1)} %all-gather.2.cloned.1.call-done, bf16[4608,256]{1,0:T(8,128)(2,1)} %param.12), kind=kOutput, calls=%fused_computation.90 | convolution fusion | flops 2415919104 | bytes 12845056 | tf_op jit(solution)/shard_map/dot_general | solution.py:118
  175.6 1.0 copy-done.5
  176.5 0.7 slice.61
  177.3 1.8 copy.88
  179.1 1.1 slice_bitcast_fusion
  180.1 1.8 fusion.38
  181.9 1.7 copy.89
  183.6 0.8 copy.90
  184.5 0.1 copy.98
  184.6 0.1 copy.97
  184.7 2.7 fusion.54
  187.4 0.1 copy.112
  187.5 0.1 copy.113
  187.7 1.5 reshape.421
  189.2 1.6 fusion.15
  190.9 0.5 copy.114
  191.4 5.1 %convolution_convert_fusion = bf16[1024,4608]{1,0:T(8,128)(2,1)} fusion(bf16[256,4608]{1,0:T(8,128)(2,1)S(1)} %copy-done, bf16[128,8,2,128]{3,2,1,0:T(2,128)(2,1)S(1)} %bitcast.138), kind=kOutput, calls=%fused_computation.2 | convolution fusion | flops 2420637696 | bytes 12320768 | tf_op jit(solution)/shard_map/dot_general | solution.py:153
  196.5 80.1 %reduce-scatter.2.cloned.1.call-done = bf16[64,4608]{1,0:T(8,128)(2,1)} async-done(((bf16[1024,4608]{1,0:T(8,128)(2,1)}), bf16[64,4608]{1,0:T(8,128)(2,1)}) %reduce-scatter.2.cloned.1.call-update) | async-done | bytes 589840 | tf_op jit(solution)/shard_map/reduce_scatter | solution.py:152
  (26 shorter events, 0.4 us)
Async XLA Ops:
  6.5 184.9 %copy-start = (bf16[256,4608]{1,0:T(8,128)(2,1)S(1)}, bf16[256,4608]{1,0:T(8,128)(2,1)}, u32[]{:S(2)}) copy-start(bf16[256,4608]{1,0:T(8,128)(2,1)} %param.13) | copy-start | bytes 7077892
  6.5 64.9 %all-gather.2.cloned.1.call-start = ((), (), s32[]{:S(2)}) async-start(), calls=%async_computation.4 | async-start | bytes 10027008 | tf_op jit(solution)/shard_map/all_gather | solution.py:114
  84.4 0.8 copy-start.1
  84.4 1.0 copy-start.3
  88.0 27.8 %all-to-all-start = ((bf16[16,64,256]{2,1,0:T(8,128)(2,1)}), bf16[16,64,256]{2,1,0:T(8,128)(2,1)}, u32[]{:S(2)}, u32[]{:S(2)}) async-start(bf16[16,64,256]{2,1,0:T(8,128)(2,1)} %convert_element_type.119), calls=%async_computation | async-start | bytes 1048576 | tf_op jit(solution)/shard_map/all_to_all | solution.py:128
  140.1 19.7 %all-to-all-start.2 = ((f32[16,1,128]{2,1,0:T(1,128)}), f32[16,1,128]{2,1,0:T(1,128)S(1)}, u32[]{:S(2)}, u32[]{:S(2)}) async-start(f32[16,1,128]{2,1,0:T(1,128)} %copy.111), calls=%async_computation.2 | async-start | bytes 16384 | tf_op jit(solution)/shard_map/all_to_all | solution.py:142
  159.8 27.9 %all-to-all-start.1 = ((bf16[16,64,256]{2,1,0:T(8,128)(2,1)}), bf16[16,64,256]{2,1,0:T(8,128)(2,1)}, u32[]{:S(2)}, u32[]{:S(2)}) async-start(bf16[16,64,256]{2,1,0:T(8,128)(2,1)} %reshape.413), calls=%async_computation.1 | async-start | bytes 1048576 | tf_op jit(solution)/shard_map/all_to_all | solution.py:138
  169.4 15.1 %copy-start.4 = (bf16[1024,2,64]{2,1,0:T(2,128)(2,1)S(1)}, bf16[1024,2,64]{2,1,0:T(2,128)(2,1)}, u32[]{:S(2)}) copy-start(bf16[1024,2,64]{2,1,0:T(2,128)(2,1)} %copy-done.3) | copy-start | bytes 786436
  169.4 15.2 %copy-start.2 = (bf16[1024,2,64]{2,1,0:T(2,128)(2,1)S(1)}, bf16[1024,2,64]{2,1,0:T(2,128)(2,1)}, u32[]{:S(2)}) copy-start(bf16[1024,2,64]{2,1,0:T(2,128)(2,1)} %copy-done.1) | copy-start | bytes 786436
  169.4 107.2 %reduce-scatter.2.cloned.1.call-start = ((), (), s32[]{:S(2)}) async-start(), calls=%async_computation.5 | async-start | bytes 10027008 | tf_op jit(solution)/shard_map/reduce_scatter | solution.py:152
  175.5 1.0 copy-start.5
Sparse Core Ops, SparseCore 0:
  9.2 62.1 all-gather.1
  196.6 79.9 reduce-scatter.1

commit v2 on v0

v2 whole, which is shorter than its diff:
```python
import math

import jax
import jax.numpy as jnp
import numpy as np
from jax import lax
from jax.experimental import pallas as pl
from jax.experimental.pallas import tpu as pltpu
from jax.sharding import PartitionSpec as P

D = 4608
HEADS = 32
HD = 128
QR = 64
HALF = QR // 2
PAGE = 256
POOL = 32
N = 16
SOFTCAP = 50.0
ROPE_BASE = 10000.0
COLS = 512
STEPS = D // COLS
MSG = 2 * QR
OMSG = MSG + 16
MESH = pl.DeviceIdType.MESH
F32 = jnp.float32
BF16 = jnp.bfloat16
SHARP = SOFTCAP * math.log2(math.e)


def tables():
    k = np.arange(HD // 2, dtype=np.float64)
    freq = (ROPE_BASE ** (-2.0 * k / HD)).astype(np.float32)
    angle = np.arange(QR, dtype=np.float64)[:, None] * freq.astype(np.float64)[None, :]
    cos = np.concatenate([np.cos(angle)] * 2, axis=1)
    sin = np.concatenate([-np.sin(angle), np.sin(angle)], axis=1)
    scale = (D // HEADS) ** -0.5 / SOFTCAP
    row = np.tile(np.concatenate([freq, freq])[None, :], (8, 1))
    return np.concatenate([cos * scale, sin * scale, cos, sin, row], axis=0).astype(np.float32)


def swap(i):
    return i + (i // 2) * (1 - 2 * (i % 2))


def turn(v, cos, sin):
    return v * cos + pltpu.roll(v, HD // 2, 1) * sin


def weights_of(scores):
    return jnp.exp2(SHARP * jnp.tanh(scores))


def dot_t(a, b):
    return lax.dot_general(a, b, (((1,), (1,)), ((), ())), preferred_element_type=F32)


def kernel(
    tok, wq_in, wkv_in, wo_in, pool_in, tgt, cnt, tail, mig, order, tab_in,
    out,
    xb, wq, wkv, wo, pool, tab, qout, qin, qrot, near_w, near_t, far_w, far_l, oout, oin, att,
    part, rx, ry, fin, turn_c, turn_s,
    cached_s, eslot, whose,
    sl, sw_s, sw_r, sy_s, sy_r, sx_s, sx_r, sq_s, sq_r, so_s, so_r, tx_s, tx_r, ty_s, ty_r,
):
    inst = lax.axis_index("inst")
    j = lax.axis_index("tp")
    z = inst // 2
    xh = inst % 2
    xl = j // 8
    y = (j // 2) % 4
    c = j % 2
    x = 2 * xh + xl

    def dev(px, py, pz, pc):
        return (pz * 2 + px // 2, (px % 2) * 8 + py * 2 + pc)

    up, down = (y + 1) % 4, (y + 3) % 4
    fx = (x + 1 + 2 * c) % 4
    bx = (x + 3 + 2 * c) % 4
    y_up, y_down = dev(x, up, z, c), dev(x, down, z, c)
    x_fwd, x_back = dev(fx, y, z, c), dev(bx, y, z, c)
    mate = dev(x, y, z, 1 - c)

    def remote(src, dst, ss, rs, to):
        return pltpu.make_async_remote_copy(
            src_ref=src, dst_ref=dst, send_sem=ss, recv_sem=rs, device_id=to, device_id_type=MESH
        )

    local = [
        pltpu.make_async_copy(tok, xb.at[pl.ds(0, QR)], sl.at[0]),
        pltpu.make_async_copy(wq_in, wq.at[c], sl.at[1]),
        pltpu.make_async_copy(wkv_in, wkv.at[c], sl.at[2]),
        pltpu.make_async_copy(tab_in, tab, sl.at[3]),
        pltpu.make_async_copy(wo_in, wo.at[pl.ds(pl.multiple_of(c * 256, 256), 256)], sl.at[4]),
        pltpu.make_async_copy(pool_in, pool, sl.at[5]),
    ]
    for copy in local:
        copy.start()

    barrier = pltpu.get_barrier_semaphore()
    for to in (y_up, y_down, x_fwd, x_back):
        pl.semaphore_signal(barrier, inc=1, device_id=to, device_id_type=MESH)

    def greet(i, carry):
        to = ((i // 4) * 2 + (i // 2) % 2, xl * 8 + y * 2 + i % 2)

        @pl.when((to[0] != inst) | (to[1] != j))
        def _():
            pl.semaphore_signal(barrier, inc=1, device_id=to, device_id_type=MESH)

        return carry

    lax.fori_loop(0, 32, greet, 0)
    pl.semaphore_wait(barrier, 35)

    def rows(k, half=None):
        if half is None:
            return pl.ds(k * QR, QR)
        return pl.ds(k * QR + half * HALF, HALF)

    def tok_half(half):
        return tok.at[pl.ds(half * HALF, HALF)]

    y_copies = [
        remote(tok_half(0), xb.at[rows(4, 0)], sy_s.at[0], sy_r.at[0], y_up),
        remote(tok_half(1), xb.at[rows(2, 1)], sy_s.at[1], sy_r.at[1], y_down),
        remote(tok_half(1), xb.at[rows(4, 1)], sy_s.at[2], sy_r.at[2], y_up),
        remote(tok_half(0), xb.at[rows(2, 0)], sy_s.at[3], sy_r.at[3], y_down),
        remote(xb.at[rows(4, 0)], xb.at[rows(6, 0)], sy_s.at[4], sy_r.at[4], y_up),
        remote(xb.at[rows(2, 1)], xb.at[rows(6, 1)], sy_s.at[5], sy_r.at[5], y_down),
    ]

    def x_copy(i, k, half):
        return remote(xb.at[rows(k, half)], xb.at[rows(k + 1, half)], sx_s.at[i], sx_r.at[i], x_fwd)

    x_copies = [
        remote(tok, xb.at[rows(1)], sx_s.at[0], sx_r.at[0], x_fwd),
        x_copy(1, 4, 0), x_copy(2, 2, 1), x_copy(3, 4, 1), x_copy(4, 2, 0), x_copy(5, 6, 0), x_copy(6, 6, 1),
    ]
    w_copies = [
        remote(wq_in, wq.at[c], sw_s.at[0], sw_r.at[0], mate),
        remote(wkv_in, wkv.at[c], sw_s.at[1], sw_r.at[1], mate),
        remote(wo_in, wo.at[pl.ds(pl.multiple_of(c * 256, 256), 256)], sw_s.at[2], sw_r.at[2], mate),
    ]

    def w_arrive(i, ref):
        pltpu.make_async_copy(ref, ref, sw_r.at[i]).wait()

    y_copies[0].start()
    y_copies[1].start()
    x_copies[0].start()
    y_copies[2].start()
    y_copies[3].start()
    w_copies[0].start()
    w_copies[1].start()
    w_copies[2].start()

    local[3].wait()
    freq = tab[pl.ds(4 * QR, 8), :]
    sign = jnp.where(lax.broadcasted_iota(jnp.int32, (8, HD), 1) < HD // 2, -1.0, 1.0)

    def request(r, end):
        cached = mig[0, r] * ((cnt[0, r] - 1) * PAGE + tail[0, r])
        cached_s[r] = cached
        angle = cached.astype(F32) * freq
        turn_c[r] = jnp.cos(angle)
        turn_s[r] = jnp.sin(angle) * sign
        return end

    lax.fori_loop(0, N, request, 0)

    def ends(t, carry):
        def one(r, state):
            end, found, who = state
            end = end + cnt[0, r]
            hit = tgt[0, r] == t
            return end, jnp.where(hit, end, found), jnp.where(hit, r, who)

        state = lax.fori_loop(0, N, one, (jnp.int32(0), jnp.int32(0), jnp.int32(0)))
        eslot[t] = state[1]
        whose[t] = state[2]
        return carry

    lax.fori_loop(0, N, ends, 0)

    def q_route(k, e):
        group, cross = k // 2, k % 2
        offset = swap(group)
        ox = x + cross * (bx - x)
        oy = (y + offset) % 4
        zs = (ox % 2) * 4 + oy
        here = (zs == z) & (xh == c) & (e == c)
        return here, dev(2 * c + xl, y, zs, e), z * 2 + ox // 2

    def q_copy(k, e, to, t):
        return remote(qout.at[k, e], qin.at[t], sq_s.at[k * 2 + e], sq_r.at[t], to)

    def q_send(k, e):
        here, to, t = q_route(k, e)

        @pl.when(here)
        def _():
            own = pltpu.make_async_copy(qout.at[k, e], qin.at[t], sl.at[6])
            own.start()
            own.wait()

        @pl.when(jnp.logical_not(here))
        def _():
            q_copy(k, e, to, t).start()

    causal = (
        lax.broadcasted_iota(jnp.int32, (MSG, QR), 0) % QR
        >= lax.broadcasted_iota(jnp.int32, (MSG, QR), 1)
    )

    def handle(k0, nb):
        span = pl.ds(k0 * QR, nb * QR)

        def per_core(e, carry):
            cq, sq = tab[pl.ds(0, QR), :], tab[pl.ds(QR, QR), :]
            q = jnp.dot(xb[span, :], wq[e], preferred_element_type=F32)
            for b in range(nb):
                for h in range(2):
                    v = q[b * QR:(b + 1) * QR, h * HD:(h + 1) * HD]
                    qout[k0 + b, e, pl.ds(h * QR, QR), :] = turn(v, cq, sq).astype(BF16)
            return carry

        def near(e, carry):
            ck, sk = tab[pl.ds(2 * QR, QR), :], tab[pl.ds(3 * QR, QR), :]
            kv = jnp.dot(xb[span, :], wkv[e], preferred_element_type=F32)
            for b in range(nb):
                keys = turn(kv[b * QR:(b + 1) * QR, :HD], ck, sk).astype(BF16)
                values = kv[b * QR:(b + 1) * QR, HD:].astype(BF16)
                s = dot_t(qout[k0 + b, e], keys)
                w = jnp.where(causal, weights_of(s), 0.0)
                near_t[k0 + b, e] = jnp.broadcast_to(jnp.sum(w, axis=1, keepdims=True), (MSG, HD))
                near_w[k0 + b, e] = jnp.dot(w.astype(BF16), values, preferred_element_type=F32)
            return carry

        lax.fori_loop(0, 2, per_core, 0)
        for b in range(nb):
            for e in range(2):
                q_send(k0 + b, e)
        lax.fori_loop(0, 2, near, 0)

    os_y, os_l = z % 4, z // 4
    os_off = (os_y - y + 4) % 4
    os_group = swap(os_off)
    os_stage = (os_group + 1) // 2
    os_cross = (xl + os_l) % 2
    os_k = os_group * 2 + os_cross

    def o_route(t):
        ox = 2 * (t % 2) + os_l
        hx = (ox + os_cross * (1 + 2 * xh)) % 4
        here = (t // 2 == z) & (hx == x) & (xh == c)
        return here, dev(hx, y, t // 2, xh)

    def o_copy(t, to):
        return remote(oout.at[t], oin.at[os_k, c], so_s.at[t], so_r.at[os_k * 2 + c], to)

    def source():
        for t in range(N):

            @pl.when(jnp.logical_not(o_route(t)[0]))
            def _():
                remote(qin.at[t], qin.at[t], sq_s.at[0], sq_r.at[t], mate).wait_recv()


        def rotate(t, carry):
            r = whose[t]
            q = qin[t].astype(F32)
            qrot[t] = turn(q, turn_c[r][0:1, :], turn_s[r][0:1, :]).astype(BF16)
            return carry

        lax.fori_loop(0, N, rotate, 0)
        col = lax.broadcasted_iota(jnp.int32, (MSG, PAGE), 1)

        def slot(i, state):
            r, p = state
            kv = pool[order[0, i]]
            s = dot_t(qrot[tgt[0, r]], kv[:, :HD])
            w = jnp.where(col < cached_s[r] - PAGE * p, weights_of(s), 0.0)
            more = jnp.full((MSG, HD), p, jnp.int32) > 0
            far_l[i + 1] = w[:, :HD] + w[:, HD:] + jnp.where(more, far_l[i], 0.0)
            pv = jnp.dot(w.astype(BF16), kv[:, HD:], preferred_element_type=F32)
            far_w[i + 1] = pv + jnp.where(more, far_w[i], 0.0)
            last = p + 1 == cnt[0, r]
            return jnp.where(last, jnp.minimum(r + 1, N - 1), r), jnp.where(last, 0, p + 1)

        def two(i, state):
            return slot(2 * i + 1, slot(2 * i, state))

        far_l[0] = jnp.zeros((MSG, HD), F32)
        far_w[0] = jnp.zeros((MSG, HD), F32)
        lax.fori_loop(0, POOL // 2, two, (jnp.int32(0), jnp.int32(0)))
        row = lax.broadcasted_iota(jnp.int32, (16, HD), 0)
        ones = jnp.ones((16, HD), BF16)

        def back(t, carry):
            i = eslot[t]
            sums = far_l[i]
            high = sums.astype(BF16)
            low = (sums - high.astype(F32)).astype(BF16)
            total = dot_t(ones, high) + dot_t(ones, low)
            total_h = total.astype(BF16).astype(F32)
            both = jnp.where(row == 0, total_h, jnp.where(row == 1, total - total_h, 0.0))
            oout[t, pl.ds(0, MSG), :] = far_w[i].astype(BF16)
            oout[t, pl.ds(MSG, 16), :] = both.astype(BF16)
            return carry

        lax.fori_loop(0, N, back, 0)
        for t in range(N):
            here, to = o_route(t)

            @pl.when(here)
            def _():
                own = pltpu.make_async_copy(oout.at[t], oin.at[os_k, c], sl.at[7])
                own.start()
                own.wait()

            @pl.when(jnp.logical_not(here))
            def _():
                o_copy(t, to).start()


    def project(k0, nb):
        for k in range(k0, k0 + nb):
            for e in range(2):

                @pl.when(jnp.logical_not(q_route(k, e)[0]))
                def _():
                    remote(oin.at[k, e], oin.at[k, e], so_s.at[0], so_r.at[k * 2 + e], mate).wait_recv()

        ones = jnp.ones((16, HD), BF16)

        for k in range(k0, k0 + nb):
            for e in range(2):
                far = oin[k, e, pl.ds(0, MSG), :].astype(F32)
                total = lax.dot_general(
                    oin[k, e, pl.ds(MSG, 16), :], ones, (((0,), (0,)), ((), ())), preferred_element_type=F32
                )
                done = ((near_w[k, e] + far) / (near_t[k, e] + total)).astype(BF16)
                att[e, 0, pl.ds(k * QR, QR), :] = done[:QR]
                att[e, 1, pl.ds(k * QR, QR), :] = done[QR:]
        span = pl.ds(k0 * QR, nb * QR)
        mixed = jnp.concatenate([att[e, h, span, :] for e in range(2) for h in range(2)], axis=1)

        def columns(n, carry):
            at = pl.ds(pl.multiple_of(n * COLS, COLS), COLS)
            part[span, at] = jnp.dot(mixed, wo[:, at], preferred_element_type=F32).astype(BF16)
            return carry

        lax.fori_loop(0, STEPS, columns, 0)

    def add(dst, dst_rows, sources):
        def columns(n, carry):
            at = pl.ds(pl.multiple_of(n * COLS, COLS), COLS)
            total = dst[dst_rows, at].astype(F32)
            for ref, its in sources:
                total = total + ref[its, at].astype(F32)
            dst[dst_rows, at] = total.astype(BF16)
            return carry

        lax.fori_loop(0, STEPS, columns, 0)

    def t_copy(i, g, half):
        src = part.at[rows(2 * g + 1, half)]
        return remote(src, rx.at[rows(g, half)], tx_s.at[i], tx_r.at[i], x_back)

    t_copies = [
        t_copy(0, 0, None), t_copy(1, 1, 1), t_copy(2, 2, 0),
        t_copy(3, 3, 0), t_copy(4, 3, 1), t_copy(5, 1, 0), t_copy(6, 2, 1),
    ]
    u_copies = [
        remote(part.at[rows(2, 1)], fin.at[0, pl.ds(HALF, HALF)], ty_s.at[0], ty_r.at[0], y_up),
        remote(part.at[rows(4, 0)], fin.at[1, pl.ds(0, HALF)], ty_s.at[1], ty_r.at[1], y_down),
        remote(part.at[rows(6, 0)], ry.at[pl.ds(0, HALF)], ty_s.at[2], ty_r.at[2], y_up),
        remote(part.at[rows(6, 1)], ry.at[pl.ds(HALF, HALF)], ty_s.at[3], ty_r.at[3], y_down),
        remote(part.at[rows(2, 0)], fin.at[0, pl.ds(0, HALF)], ty_s.at[4], ty_r.at[4], y_up),
        remote(part.at[rows(4, 1)], fin.at[1, pl.ds(HALF, HALF)], ty_s.at[5], ty_r.at[5], y_down),
    ]

    y_copies[0].wait_recv()
    x_copies[1].start()
    y_copies[4].start()
    y_copies[1].wait_recv()
    x_copies[2].start()
    y_copies[5].start()

    for i in range(3):
        local[i].wait()
    w_arrive(0, wq.at[1 - c])
    w_arrive(1, wkv.at[1 - c])
    x_copies[0].wait_recv()
    handle(0, 2)

    y_copies[2].wait_recv()
    x_copies[3].start()
    y_copies[3].wait_recv()
    x_copies[4].start()
    local[4].wait()
    local[5].wait()

    @pl.when(os_stage == 0)
    def _():
        source()

    y_copies[4].wait_recv()
    x_copies[5].start()
    y_copies[5].wait_recv()
    x_copies[6].start()
    for i in range(1, 5):
        x_copies[i].wait_recv()
    handle(2, 4)
    x_copies[5].wait_recv()
    x_copies[6].wait_recv()
    handle(6, 2)

    @pl.when(os_stage != 0)
    def _():
        source()

    w_arrive(2, wo.at[pl.ds(pl.multiple_of((1 - c) * 256, 256), 256)])
    project(0, 2)
    t_copies[0].start()
    project(2, 4)
    t_copies[1].start()
    t_copies[2].start()
    project(6, 2)
    for i in range(3, 7):
        t_copies[i].start()

    t_copies[0].wait_recv()
    t_copies[1].wait_recv()
    add(part, rows(2, 1), [(rx, rows(1, 1))])
    u_copies[0].start()
    t_copies[2].wait_recv()
    add(part, rows(4, 0), [(rx, rows(2, 0))])
    u_copies[1].start()
    t_copies[3].wait_recv()
    add(part, rows(6, 0), [(rx, rows(3, 0))])
    u_copies[2].start()
    t_copies[4].wait_recv()
    add(part, rows(6, 1), [(rx, rows(3, 1))])
    u_copies[3].start()
    t_copies[5].wait_recv()
    u_copies[2].wait_recv()
    add(part, rows(2, 0), [(rx, rows(1, 0)), (ry, pl.ds(0, HALF))])
    u_copies[4].start()
    t_copies[6].wait_recv()
    u_copies[3].wait_recv()
    add(part, rows(4, 1), [(rx, rows(2, 1)), (ry, pl.ds(HALF, HALF))])
    u_copies[5].start()
    u_copies[0].wait_recv()
    u_copies[1].wait_recv()
    u_copies[4].wait_recv()
    u_copies[5].wait_recv()

    def finish(n, carry):
        at = pl.ds(pl.multiple_of(n * COLS, COLS), COLS)
        total = part[pl.ds(0, QR), at].astype(F32) + rx[pl.ds(0, QR), at].astype(F32)
        total = total + fin[0, :, at].astype(F32) + fin[1, :, at].astype(F32)
        out[:, at] = total.astype(BF16)
        return carry

    lax.fori_loop(0, STEPS, finish, 0)

    for copy in y_copies + x_copies + w_copies + t_copies + u_copies:
        copy.wait_send()

    for i in range(N):
        here, to, t = q_route(i // 2, i % 2)

        @pl.when(jnp.logical_not(here))
        def _():
            q_copy(i // 2, i % 2, to, t).wait_send()

        back_here, back_to = o_route(i)

        @pl.when(jnp.logical_not(back_here))
        def _():
            o_copy(i, back_to).wait_send()


def shards(tokens, w_query, w_keyval, w_out, kv_pool, req_target, page_counts, tail_tokens, migrate, pool_order):
    table = jnp.asarray(tables())
    anyspace = pl.BlockSpec(memory_space=pl.ANY)
    smem = pl.BlockSpec(memory_space=pltpu.SMEM)
    dma = pltpu.SemaphoreType.DMA
    return pl.pallas_call(
        kernel,
        out_shape=jax.ShapeDtypeStruct((QR, D), BF16),
        in_specs=[anyspace] * 5 + [smem] * 5 + [anyspace],
        out_specs=pl.BlockSpec(memory_space=pltpu.VMEM),
        scratch_shapes=[
            pltpu.VMEM((8 * QR, D), BF16),
            pltpu.VMEM((2, D, 256), BF16),
            pltpu.VMEM((2, D, 256), BF16),
            pltpu.VMEM((512, D), BF16),
            pltpu.VMEM((POOL, PAGE, 256), BF16),
            pltpu.VMEM((4 * QR + 8, HD), F32),
            pltpu.VMEM((8, 2, MSG, HD), BF16),
            pltpu.VMEM((N, MSG, HD), BF16),
            pltpu.VMEM((N, MSG, HD), BF16),
            pltpu.VMEM((8, 2, MSG, HD), F32),
            pltpu.VMEM((8, 2, MSG, HD), F32),
            pltpu.VMEM((POOL + 1, MSG, HD), F32),
            pltpu.VMEM((POOL + 1, MSG, HD), F32),
            pltpu.VMEM((N, OMSG, HD), BF16),
            pltpu.VMEM((8, 2, OMSG, HD), BF16),
            pltpu.VMEM((2, 2, 8 * QR, HD), BF16),
            pltpu.VMEM((8 * QR, D), BF16),
            pltpu.VMEM((4 * QR, D), BF16),
            pltpu.VMEM((QR, D), BF16),
            pltpu.VMEM((2, QR, D), BF16),
            pltpu.VMEM((N, 8, HD), F32),
            pltpu.VMEM((N, 8, HD), F32),
            pltpu.SMEM((N,), jnp.int32),
            pltpu.SMEM((N,), jnp.int32),
            pltpu.SMEM((N,), jnp.int32),
            dma((8,)),
            dma((3,)), dma((3,)),
            dma((6,)), dma((6,)),
            dma((7,)), dma((7,)),
            dma((N,)), dma((N,)),
            dma((N,)), dma((N,)),
            dma((7,)), dma((7,)),
            dma((6,)), dma((6,)),
        ],
        compiler_params=pltpu.CompilerParams(
            collective_id=0, has_side_effects=True, vmem_limit_bytes=58 * 2**20
        ),
        cost_estimate=pl.CostEstimate(flops=9 * 10**9, bytes_accessed=13 * 10**6, transcendentals=3 * 10**6),
    )(tokens, w_query, w_keyval, w_out, kv_pool, req_target, page_counts, tail_tokens, migrate, pool_order, table)


def solution(mesh):
    return jax.shard_map(
        shards,
        mesh=mesh,
        in_specs=(
            P(("inst", "tp"), None),
            P(None, "tp"),
            P(None, "tp"),
            P("tp", None),
            P("inst", None, "tp"),
            P("inst", None),
            P("inst", None),
            P("inst", None),
            P("inst", None),
            P("inst", None),
        ),
        out_specs=P(("inst", "tp"), None),
        check_vma=False,
    )
```

time: 396 us -> 122 us (0.31)
  the two profiles are of different devices: /device:TPU:32 before, /device:TPU:82 now
where the time goes in v2:
time: 122 us
  Pallas kernels  120 us (98%)
  local copies, waits for them, and re-layouts  1.92 us (2%)
    pallas_call x1, Pallas kernels, shards(): pl.pallas_call(kernel, out_shape=jax.ShapeDtypeStruct((QR, D), BF16), in_...  120 us

profile of v2, /device:TPU:82, one launch (start us, length us, event | category | flops | bytes accessed | tf_op | source)
XLA Modules:
  0.0 121.8 jit_solution(17294888241932563909)
XLA Ops:
  0.0 119.8 %shard_map.109 = bf16[64,4608]{1,0:T(8,128)(2,1)} custom-call(bf16[64,4608]{1,0:T(8,128)(2,1)} %tok.1, bf16[4608,256]{1,0:T(8,128)(2,1)} %wq_in.1, bf16[4608,256]{1,0:T(8,128)(2,1)} %wkv_in.1, bf16[256,4608]{1,0:T(8,128)(2,1)} %wo_in.1, bf16[32,256,256]{2,1,0:T(8,128)(2,1)} %pool_in.1, s32[1,16]{1,0:T(1,128)} %tgt.1, s32[1,16]{1,0:T(1,128)} %cnt.1, ...), custom_call_target="tpu_custom_call" | custom-call | flops 8999999488 | bytes 13000000 | tf_op jit(solution)/shard_map/pallas_call | solution.py:492
  119.9 1.9 %copy.13 = bf16[64,4608]{1,0:T(8,128)(2,1)} copy(bf16[64,4608]{1,0:T(8,128)(2,1)} %shard_map.109) | data formatting | bytes 1179648

commit v3 on v2

--- a/solution.py
+++ b/solution.py
@@ -22,6 +22,7 @@
 STEPS = D // COLS
 MSG = 2 * QR
 OMSG = MSG + 16
+BATCH = 8
 MESH = pl.DeviceIdType.MESH
 F32 = jnp.float32
 BF16 = jnp.bfloat16
@@ -274,27 +275,38 @@
             qrot[t] = turn(q, turn_c[r][0:1, :], turn_s[r][0:1, :]).astype(BF16)
             return carry
 
-        lax.fori_loop(0, N, rotate, 0)
+        lax.fori_loop(0, N, rotate, 0, unroll=4)
         col = lax.broadcasted_iota(jnp.int32, (MSG, PAGE), 1)
 
-        def slot(i, state):
+        def slots(i, state):
             r, p = state
-            kv = pool[order[0, i]]
-            s = dot_t(qrot[tgt[0, r]], kv[:, :HD])
-            w = jnp.where(col < cached_s[r] - PAGE * p, weights_of(s), 0.0)
-            more = jnp.full((MSG, HD), p, jnp.int32) > 0
-            far_l[i + 1] = w[:, :HD] + w[:, HD:] + jnp.where(more, far_l[i], 0.0)
-            pv = jnp.dot(w.astype(BF16), kv[:, HD:], preferred_element_type=F32)
-            far_w[i + 1] = pv + jnp.where(more, far_w[i], 0.0)
-            last = p + 1 == cnt[0, r]
-            return jnp.where(last, jnp.minimum(r + 1, N - 1), r), jnp.where(last, 0, p + 1)
-
-        def two(i, state):
-            return slot(2 * i + 1, slot(2 * i, state))
+            owner, page = [], []
+            for u in range(BATCH):
+                owner.append(r)
+                page.append(p)
+                last = p + 1 == cnt[0, r]
+                r, p = jnp.where(last, jnp.minimum(r + 1, N - 1), r), jnp.where(last, 0, p + 1)
+            kv = [pool[order[0, BATCH * i + u]] for u in range(BATCH)]
+            s = [dot_t(qrot[tgt[0, owner[u]]], kv[u][:, :HD]) for u in range(BATCH)]
+            w = [
+                jnp.where(col < cached_s[owner[u]] - PAGE * page[u], weights_of(s[u]), 0.0)
+                for u in range(BATCH)
+            ]
+            pv = [
+                jnp.dot(w[u].astype(BF16), kv[u][:, HD:], preferred_element_type=F32) for u in range(BATCH)
+            ]
+            sum_l, sum_w = far_l[BATCH * i], far_w[BATCH * i]
+            for u in range(BATCH):
+                more = jnp.full((MSG, HD), page[u], jnp.int32) > 0
+                sum_l = w[u][:, :HD] + w[u][:, HD:] + jnp.where(more, sum_l, 0.0)
+                sum_w = pv[u] + jnp.where(more, sum_w, 0.0)
+                far_l[BATCH * i + u + 1] = sum_l
+                far_w[BATCH * i + u + 1] = sum_w
+            return r, p
 
         far_l[0] = jnp.zeros((MSG, HD), F32)
         far_w[0] = jnp.zeros((MSG, HD), F32)
-        lax.fori_loop(0, POOL // 2, two, (jnp.int32(0), jnp.int32(0)))
+        lax.fori_loop(0, POOL // BATCH, slots, (jnp.int32(0), jnp.int32(0)))
         row = lax.broadcasted_iota(jnp.int32, (16, HD), 0)
         ones = jnp.ones((16, HD), BF16)
 
@@ -310,7 +322,7 @@
             oout[t, pl.ds(MSG, 16), :] = both.astype(BF16)
             return carry
 
-        lax.fori_loop(0, N, back, 0)
+        lax.fori_loop(0, N, back, 0, unroll=4)
         for t in range(N):
             here, to = o_route(t)
 

time: 122 us -> 110 us (0.902)
  Pallas kernels: 120 us -> 108 us
    pallas_call x1, Pallas kernels: 120 us -> 108 us  [shards(): pl.pallas_call(kernel, out_shape=jax.ShapeDtypeStruct((QR, D), BF16), in_...]
where the time goes in v3:
time: 110 us
  Pallas kernels  108 us (98%)
  local copies, waits for them, and re-layouts  1.92 us (2%)
    pallas_call x1, Pallas kernels, shards(): pl.pallas_call(kernel, out_shape=jax.ShapeDtypeStruct((QR, D), BF16), in_...  108 us

profile of v3, /device:TPU:82, one launch (start us, length us, event | category | flops | bytes accessed | tf_op | source)
XLA Modules:
  0.0 109.8 jit_solution(16937793293846685732)
XLA Ops:
  0.0 107.9 %shard_map.109 = bf16[64,4608]{1,0:T(8,128)(2,1)} custom-call(bf16[64,4608]{1,0:T(8,128)(2,1)} %tok.1, bf16[4608,256]{1,0:T(8,128)(2,1)} %wq_in.1, bf16[4608,256]{1,0:T(8,128)(2,1)} %wkv_in.1, bf16[256,4608]{1,0:T(8,128)(2,1)} %wo_in.1, bf16[32,256,256]{2,1,0:T(8,128)(2,1)} %pool_in.1, s32[1,16]{1,0:T(1,128)} %tgt.1, s32[1,16]{1,0:T(1,128)} %cnt.1, ...), custom_call_target="tpu_custom_call" | custom-call | flops 8999999488 | bytes 13000000 | tf_op jit(solution)/shard_map/pallas_call | solution.py:504
  107.9 1.9 %copy.13 = bf16[64,4608]{1,0:T(8,128)(2,1)} copy(bf16[64,4608]{1,0:T(8,128)(2,1)} %shard_map.109) | data formatting | bytes 1179648

commit v4 on v3

--- a/solution.py
+++ b/solution.py
@@ -124,20 +124,20 @@
         return tok.at[pl.ds(half * HALF, HALF)]
 
     y_copies = [
-        remote(tok_half(0), xb.at[rows(4, 0)], sy_s.at[0], sy_r.at[0], y_up),
-        remote(tok_half(1), xb.at[rows(2, 1)], sy_s.at[1], sy_r.at[1], y_down),
-        remote(tok_half(1), xb.at[rows(4, 1)], sy_s.at[2], sy_r.at[2], y_up),
-        remote(tok_half(0), xb.at[rows(2, 0)], sy_s.at[3], sy_r.at[3], y_down),
-        remote(xb.at[rows(4, 0)], xb.at[rows(6, 0)], sy_s.at[4], sy_r.at[4], y_up),
-        remote(xb.at[rows(2, 1)], xb.at[rows(6, 1)], sy_s.at[5], sy_r.at[5], y_down),
+        remote(tok_half(0), xb.at[rows(2, 0)], sy_s.at[0], sy_r.at[0], y_up),
+        remote(tok_half(1), xb.at[rows(1, 1)], sy_s.at[1], sy_r.at[1], y_down),
+        remote(tok_half(1), xb.at[rows(2, 1)], sy_s.at[2], sy_r.at[2], y_up),
+        remote(tok_half(0), xb.at[rows(1, 0)], sy_s.at[3], sy_r.at[3], y_down),
+        remote(xb.at[rows(2, 0)], xb.at[rows(3, 0)], sy_s.at[4], sy_r.at[4], y_up),
+        remote(xb.at[rows(1, 1)], xb.at[rows(3, 1)], sy_s.at[5], sy_r.at[5], y_down),
     ]
 
     def x_copy(i, k, half):
-        return remote(xb.at[rows(k, half)], xb.at[rows(k + 1, half)], sx_s.at[i], sx_r.at[i], x_fwd)
+        return remote(xb.at[rows(k, half)], xb.at[rows(k + 4, half)], sx_s.at[i], sx_r.at[i], x_fwd)
 
     x_copies = [
-        remote(tok, xb.at[rows(1)], sx_s.at[0], sx_r.at[0], x_fwd),
-        x_copy(1, 4, 0), x_copy(2, 2, 1), x_copy(3, 4, 1), x_copy(4, 2, 0), x_copy(5, 6, 0), x_copy(6, 6, 1),
+        remote(tok, xb.at[rows(4)], sx_s.at[0], sx_r.at[0], x_fwd),
+        x_copy(1, 2, 0), x_copy(2, 1, 1), x_copy(3, 2, 1), x_copy(4, 1, 0), x_copy(5, 3, 0), x_copy(6, 3, 1),
     ]
     w_copies = [
         remote(wq_in, wq.at[c], sw_s.at[0], sw_r.at[0], mate),
@@ -186,7 +186,7 @@
     lax.fori_loop(0, N, ends, 0)
 
     def q_route(k, e):
-        group, cross = k // 2, k % 2
+        group, cross = k % 4, k // 4
         offset = swap(group)
         ox = x + cross * (bx - x)
         oy = (y + offset) % 4
@@ -250,7 +250,7 @@
     os_group = swap(os_off)
     os_stage = (os_group + 1) // 2
     os_cross = (xl + os_l) % 2
-    os_k = os_group * 2 + os_cross
+    os_k = os_group + 4 * os_cross
 
     def o_route(t):
         ox = 2 * (t % 2) + os_l
@@ -378,7 +378,7 @@
         lax.fori_loop(0, STEPS, columns, 0)
 
     def t_copy(i, g, half):
-        src = part.at[rows(2 * g + 1, half)]
+        src = part.at[rows(g + 4, half)]
         return remote(src, rx.at[rows(g, half)], tx_s.at[i], tx_r.at[i], x_back)
 
     t_copies = [
@@ -386,12 +386,12 @@
         t_copy(3, 3, 0), t_copy(4, 3, 1), t_copy(5, 1, 0), t_copy(6, 2, 1),
     ]
     u_copies = [
-        remote(part.at[rows(2, 1)], fin.at[0, pl.ds(HALF, HALF)], ty_s.at[0], ty_r.at[0], y_up),
-        remote(part.at[rows(4, 0)], fin.at[1, pl.ds(0, HALF)], ty_s.at[1], ty_r.at[1], y_down),
-        remote(part.at[rows(6, 0)], ry.at[pl.ds(0, HALF)], ty_s.at[2], ty_r.at[2], y_up),
-        remote(part.at[rows(6, 1)], ry.at[pl.ds(HALF, HALF)], ty_s.at[3], ty_r.at[3], y_down),
-        remote(part.at[rows(2, 0)], fin.at[0, pl.ds(0, HALF)], ty_s.at[4], ty_r.at[4], y_up),
-        remote(part.at[rows(4, 1)], fin.at[1, pl.ds(HALF, HALF)], ty_s.at[5], ty_r.at[5], y_down),
+        remote(part.at[rows(1, 1)], fin.at[0, pl.ds(HALF, HALF)], ty_s.at[0], ty_r.at[0], y_up),
+        remote(part.at[rows(2, 0)], fin.at[1, pl.ds(0, HALF)], ty_s.at[1], ty_r.at[1], y_down),
+        remote(part.at[rows(3, 0)], ry.at[pl.ds(0, HALF)], ty_s.at[2], ty_r.at[2], y_up),
+        remote(part.at[rows(3, 1)], ry.at[pl.ds(HALF, HALF)], ty_s.at[3], ty_r.at[3], y_down),
+        remote(part.at[rows(1, 0)], fin.at[0, pl.ds(0, HALF)], ty_s.at[4], ty_r.at[4], y_up),
+        remote(part.at[rows(2, 1)], fin.at[1, pl.ds(HALF, HALF)], ty_s.at[5], ty_r.at[5], y_down),
     ]
 
     y_copies[0].wait_recv()
@@ -405,66 +405,64 @@
         local[i].wait()
     w_arrive(0, wq.at[1 - c])
     w_arrive(1, wkv.at[1 - c])
+    handle(0, 1)
     x_copies[0].wait_recv()
-    handle(0, 2)
+    handle(4, 1)
 
     y_copies[2].wait_recv()
     x_copies[3].start()
     y_copies[3].wait_recv()
     x_copies[4].start()
+    handle(1, 2)
     local[4].wait()
     local[5].wait()
-
-    @pl.when(os_stage == 0)
-    def _():
-        source()
 
     y_copies[4].wait_recv()
     x_copies[5].start()
     y_copies[5].wait_recv()
     x_copies[6].start()
+    handle(3, 1)
     for i in range(1, 5):
         x_copies[i].wait_recv()
-    handle(2, 4)
+    handle(5, 2)
     x_copies[5].wait_recv()
     x_copies[6].wait_recv()
-    handle(6, 2)
-
-    @pl.when(os_stage != 0)
-    def _():
-        source()
+    handle(7, 1)
+
+    source()
 
     w_arrive(2, wo.at[pl.ds(pl.multiple_of((1 - c) * 256, 256), 256)])
-    project(0, 2)
-    t_copies[0].start()
-    project(2, 4)
+    project(5, 2)
     t_copies[1].start()
     t_copies[2].start()
-    project(6, 2)
+    project(7, 1)
     for i in range(3, 7):
         t_copies[i].start()
-
-    t_copies[0].wait_recv()
+    project(4, 1)
+    t_copies[0].start()
+    project(0, 4)
+
     t_copies[1].wait_recv()
-    add(part, rows(2, 1), [(rx, rows(1, 1))])
+    add(part, rows(1, 1), [(rx, rows(1, 1))])
     u_copies[0].start()
     t_copies[2].wait_recv()
-    add(part, rows(4, 0), [(rx, rows(2, 0))])
+    add(part, rows(2, 0), [(rx, rows(2, 0))])
     u_copies[1].start()
     t_copies[3].wait_recv()
-    add(part, rows(6, 0), [(rx, rows(3, 0))])
+    add(part, rows(3, 0), [(rx, rows(3, 0))])
     u_copies[2].start()
     t_copies[4].wait_recv()
-    add(part, rows(6, 1), [(rx, rows(3, 1))])
+    add(part, rows(3, 1), [(rx, rows(3, 1))])
     u_copies[3].start()
     t_copies[5].wait_recv()
     u_copies[2].wait_recv()
-    add(part, rows(2, 0), [(rx, rows(1, 0)), (ry, pl.ds(0, HALF))])
+    add(part, rows(1, 0), [(rx, rows(1, 0)), (ry, pl.ds(0, HALF))])
     u_copies[4].start()
     t_copies[6].wait_recv()
     u_copies[3].wait_recv()
-    add(part, rows(4, 1), [(rx, rows(2, 1)), (ry, pl.ds(HALF, HALF))])
+    add(part, rows(2, 1), [(rx, rows(2, 1)), (ry, pl.ds(HALF, HALF))])
     u_copies[5].start()
+    t_copies[0].wait_recv()
     u_copies[0].wait_recv()
     u_copies[1].wait_recv()
     u_copies[4].wait_recv()

time: 110 us -> 106 us (0.964)
  the two profiles are of different devices: /device:TPU:82 before, /device:TPU:32 now
where the time goes in v4:
time: 106 us; the launch traced here: 105 us
  Pallas kernels  103 us (97%)
  local copies, waits for them, and re-layouts  1.92 us (2%)
    pallas_call x1, Pallas kernels, shards(): pl.pallas_call(kernel, out_shape=jax.ShapeDtypeStruct((QR, D), BF16), in_...  103 us

profile of v4, /device:TPU:32, one launch (start us, length us, event | category | flops | bytes accessed | tf_op | source)
XLA Modules:
  0.0 104.6 jit_solution(10499145087444706989)
XLA Ops:
  0.0 102.6 %shard_map.109 = bf16[64,4608]{1,0:T(8,128)(2,1)} custom-call(bf16[64,4608]{1,0:T(8,128)(2,1)} %tok.1, bf16[4608,256]{1,0:T(8,128)(2,1)} %wq_in.1, bf16[4608,256]{1,0:T(8,128)(2,1)} %wkv_in.1, bf16[256,4608]{1,0:T(8,128)(2,1)} %wo_in.1, bf16[32,256,256]{2,1,0:T(8,128)(2,1)} %pool_in.1, s32[1,16]{1,0:T(1,128)} %tgt.1, s32[1,16]{1,0:T(1,128)} %cnt.1, ...), custom_call_target="tpu_custom_call" | custom-call | flops 8999999488 | bytes 13000000 | tf_op jit(solution)/shard_map/pallas_call | solution.py:502
  102.6 1.9 %copy.13 = bf16[64,4608]{1,0:T(8,128)(2,1)} copy(bf16[64,4608]{1,0:T(8,128)(2,1)} %shard_map.109) | data formatting | bytes 1179648
